TPU v7x, 32 devices: a whole 2x2x4 slice. The times are simulated.
32 devices in a mesh: sec: 4 (over z), blk: 8 (over y, x, core).
Axes of the slice: x: 2, y: 2, z: 4, core: 2. Of those that a mesh axis runs over, the one named last changes fastest.
Arguments:
- guess: bfloat16 [4, 8, 128, 8, 128], P('sec', None, None, 'blk'), may hold values from -6 to 6
- left_env: bfloat16 [4, 2, 8, 128, 128], P('sec', None, 'blk'), as said below
- right_env: bfloat16 [4, 2, 8, 128, 128], P('sec', None, 'blk'), as said below
- left_dims: int32 [4, 8], P('sec'), may hold values from 1 to 128, as said below
- right_dims: int32 [4, 8], P('sec'), may hold values from 1 to 128, as said below
- left_labels: int32 [4, 8], P('sec'), may hold values from 0 to 4, as said below
- right_labels: int32 [4, 8], P('sec'), may hold values from 0 to 4, as said below
Outputs:
- waves: float32 [4, 8, 128, 8, 128], P('sec', None, None, 'blk')
- energies: float32 [4, 2], P('sec')
Inputs may be any that keep to these rules, and one draw needn't show every extreme that they name: `left_env`: every block of the environments is symmetric in its last two dimensions. `right_env`: every block of the environments is symmetric in its last two dimensions. `left_dims`: some sector of every section has all 128 states live. The left sectors of section s are the right sectors of section s - 1, with the same sizes. `right_dims`: some sector of every section has all 128 states live. `left_labels`: the left labels of section s are the right labels of section s - 1. Every particle number from 0 to 4 labels some sector of every bond. `right_labels`: every particle number from 0 to 4 labels some sector of every bond.
All inputs are finite; a program needn't handle non-finite values.
Results may differ from a plain program's by a relative error of at most 0.012.
Values may be sent and summed in bfloat16 or wider, within the bound.
A program may use at most 64 MiB of HBM per device.

v0:
```python
import jax
import jax.numpy as jnp
from jax import lax
from jax.sharding import PartitionSpec as P

ITERS = 2


EPS = 1e-06


def from_behind(block, axis, distance):
    devices = range(lax.axis_size(axis))
    route = [(i - distance, i) for i in devices if i - distance in devices]
    return lax.ppermute(block, axis, route)


def block_mask(left_sizes, right_sizes, left_marks, right_marks, block_size):
    total = left_marks[:, None] + right_marks[None, :]
    allowed = (total == 4).astype(jnp.float32)
    offsets = jnp.arange(block_size, dtype=jnp.int32)
    live_rows = (offsets[None, :] < left_sizes[:, None]).astype(jnp.float32)
    live_cols = (offsets[None, :] < right_sizes[:, None]).astype(jnp.float32)
    return allowed[:, None, :, None] * live_rows[:, :, None, None] * live_cols[None, None, :, :]


def left_product(left_block):
    gathered = lax.all_gather(left_block, "blk", axis=1, tiled=True)

    def product(rounded):
        return jnp.einsum(
            "wqac,qcrb->wqarb", gathered, rounded, preferred_element_type=jnp.float32
        ).astype(jnp.bfloat16)

    return product


def hamiltonian(product, right_block, pattern):

    def apply_all(vector):
        left_done = product(vector.astype(jnp.bfloat16))
        return (
            jnp.einsum(
                "wqarc,wrbc->qarb", left_done, right_block, preferred_element_type=jnp.float32
            )
            * pattern
        )

    return apply_all


def davidson(start, apply_all, pattern):
    vector = start * pattern
    total = lax.psum(jnp.sum(vector * vector), "blk")
    vector = vector / jnp.sqrt(total + EPS)
    image = apply_all(vector)
    ritz_value = lax.psum(jnp.sum(vector * image), "blk")
    for sweep in range(ITERS):
        residual = image - ritz_value * vector
        squared = lax.psum(jnp.sum(residual * residual), "blk") + EPS
        response = apply_all(residual)
        correlation = lax.psum(jnp.sum(residual * response), "blk")
        coupling = correlation / squared
        midpoint = 0.5 * (ritz_value - coupling)
        radius = jnp.sqrt(midpoint * midpoint + squared)
        cosine = jnp.sqrt(0.5 * (1.0 - midpoint / radius))
        sine_value = -jnp.sqrt(0.5 * (1.0 + midpoint / radius))
        length = jnp.sqrt(squared)
        vector = cosine * vector + sine_value / length * residual
        image = cosine * image + sine_value / length * response
        ritz_value = 0.5 * (ritz_value + coupling) - radius
    return (vector, ritz_value)


def refresh(vector, product, states):
    rounded = vector.astype(jnp.bfloat16)
    left_done = product(rounded)
    return (
        states
        * jnp.einsum("qarb,wqarc->wrbc", rounded, left_done, preferred_element_type=jnp.float32)
    ).astype(jnp.bfloat16)


def local(guess, left_env, right_env, left_dims, right_dims, left_labels, right_labels):
    start_guess = guess[0].astype(jnp.float32)
    left_block = left_env[0]
    right_block = right_env[0]
    sector_count = start_guess.shape[0]
    block_size = start_guess.shape[1]
    owned_count = start_guess.shape[2]
    states = sector_count * block_size
    first_owned = lax.axis_index("blk") * owned_count
    owned_sizes = lax.dynamic_slice_in_dim(right_dims[0], first_owned, owned_count, 0)
    owned_marks = lax.dynamic_slice_in_dim(right_labels[0], first_owned, owned_count, 0)
    pattern = block_mask(left_dims[0], owned_sizes, left_labels[0], owned_marks, block_size)
    first_product = left_product(left_block)
    first_vector, first_energy = davidson(
        start_guess, hamiltonian(first_product, right_block, pattern), pattern
    )
    fresh = refresh(first_vector, first_product, states)
    passed = from_behind(fresh, "sec", 1)
    second_left = jnp.where(lax.axis_index("sec") == 0, left_block, passed)
    second_product = left_product(second_left)
    second_vector, second_energy = davidson(
        first_vector, hamiltonian(second_product, right_block, pattern), pattern
    )
    waves = (states * second_vector)[None]
    energies = jnp.stack([first_energy, second_energy])[None]
    return (waves, energies)


def solution(mesh):
    return jax.shard_map(
        local,
        mesh=mesh,
        in_specs=(
            P("sec", None, None, "blk", None),
            P("sec", None, "blk", None, None),
            P("sec", None, "blk", None, None),
            P("sec", None),
            P("sec", None),
            P("sec", None),
            P("sec", None),
        ),
        out_specs=(P("sec", None, None, "blk", None), P("sec", None)),
        check_vma=False,
    )
```

profile of v0, /device:TPU:9, one launch (start us, length us, event | category | flops | bytes accessed | tf_op | source)
XLA Modules:
  0.0 160.9 jit_solution(114007146329257892)
XLA Ops:
  0.6 0.0 copy-start
  0.6 0.0 copy-start.3
  0.7 0.0 copy-start.4
  0.7 0.7 copy-done.3
  1.3 0.0 copy-done.4
  1.4 0.6 constant_dynamic-slice_fusion
  1.9 0.6 compare_convert_fusion
  2.6 0.0 copy-start.6
  2.6 0.6 copy-done.6
  3.3 0.6 fusion.73
  3.9 0.0 copy-start.5
  3.9 0.6 copy-done.5
  4.6 0.1 fusion.72
  4.6 0.0 copy-start.2
  4.6 1.8 %fusion.18 = f32[]{:T(128)} fusion(bf16[1,8,128,1,128]{4,2,3,1,0:T(8,128)(2,1)} %param.7, f32[128]{0:T(128)S(1)} %compare_convert_fusion, f32[8,128]{1,0:T(8,128)S(1)} %fusion.72), kind=kLoop, calls=%fused_computation.41 | loop fusion | flops 655359 | bytes 266756 | tf_op jit(solution)/shard_map/reduce_sum | solution.py:54
  6.4 12.4 %psum.84 = f32[]{:T(128)} all-reduce(f32[]{:T(128)} %fusion.18), channel_id=1, replica_groups=mesh['sec'=4,'blk'=8] {'blk'}, use_global_device_ids=true, to_apply=%region_1.0 | all-reduce | flops 1 | bytes 8 | tf_op jit(solution)/shard_map/psum | solution.py:54
  19.6 0.0 copy-done.2
  19.6 0.0 copy-start.1
  19.6 11.4 %all-gather = bf16[1,2,8,128,128]{4,3,1,0,2:T(8,128)(2,1)S(1)} all-gather(bf16[1,2,1,128,128]{4,3,1,0,2:T(8,128)(2,1)S(1)} %bitcast.356), channel_id=2, replica_groups=mesh['sec'=4,'blk'=8] {'blk'}, dimensions={2}, use_global_device_ids=true | all-gather | bytes 589824 | tf_op jit(solution)/shard_map/all_gather | solution.py:28
  30.9 0.0 copy-done
  30.9 0.0 copy-done.1
  30.9 1.6 multiply_reduce_fusion.8
  32.5 12.0 %psum.85 = f32[]{:T(128)} all-reduce(f32[]{:T(128)} %get-tuple-element.24), channel_id=1, replica_groups=mesh['sec'=4,'blk'=8] {'blk'}, use_global_device_ids=true, to_apply=%region_3.0 | all-reduce | flops 1 | bytes 8 | tf_op jit(solution)/shard_map/psum | solution.py:57
  44.5 2.3 %multiply_reduce_fusion.6 = (f32[]{:T(128)}, f32[]{:T(128)}, f32[8,128,1,128]{3,1,0,2:T(8,128)S(1)}) fusion(f32[8,128,1,128]{3,1,0,2:T(8,128)S(1)} %get-tuple-element.25, f32[]{:T(128)} %psum.85, f32[]{:T(128)S(6)} %sqrt.54, f32[128]{0:T(128)S(1)} %compare_convert_fusion, f32[8,128]{1,0:T(8,128)S(1)} %fusion.72, ...), kind=kOutput, calls=%fused_computation.62 | convolution fusion | flops 136839168 | bytes 1905168 | tf_op jit(solution)/shard_map/wqarc,wrbc->qarb/dot_general | solution.py:43
  46.8 13.8 %all-reduce.3 = (f32[]{:T(128)}, f32[]{:T(128)}) all-reduce(f32[]{:T(128)} %get-tuple-element.9, f32[]{:T(128)} %get-tuple-element.8), channel_id=1, replica_groups=mesh['sec'=4,'blk'=8] {'blk'}, use_global_device_ids=true, to_apply=%region_5.0 | all-reduce | flops 2 | bytes 16 | tf_op jit(solution)/shard_map/psum | solution.py:62
  63.3 1.6 multiply_reduce_fusion.5
  64.9 1.3 fusion.14
  66.2 12.5 %all-reduce.2 = (f32[]{:T(128)}, f32[]{:T(128)}) all-reduce(f32[]{:T(128)} %fusion.14, f32[]{:T(128)} %get-tuple-element.22), channel_id=1, replica_groups=mesh['sec'=4,'blk'=8] {'blk'}, use_global_device_ids=true, to_apply=%region_9.0 | all-reduce | flops 2 | bytes 16 | tf_op jit(solution)/shard_map/psum | solution.py:62
  80.3 1.6 multiply_reduce_fusion.4
  81.8 0.5 fusion.13
  82.3 3.2 %collective-permute-start = (bf16[2,1,128,128]{2,3,0,1:T(8,128)(2,1)S(1)}, bf16[2,1,128,128]{2,3,0,1:T(8,128)(2,1)S(1)}, u32[]{:S(2)}, u32[]{:S(2)}) collective-permute-start(bf16[2,1,128,128]{2,3,0,1:T(8,128)(2,1)S(1)} %fusion.13), channel_id=1, source_target_pairs={{0,8},{8,16},{16,24},{1,9},{9,17},{17,25},{2,10},{10,18},{18,26},{... | collective-permute-start | bytes 196616 | tf_op jit(solution)/shard_map/ppermute | solution.py:15
  85.5 12.7 %psum.90 = f32[]{:T(128)} all-reduce(f32[]{:T(128)} %get-tuple-element.20), channel_id=1, replica_groups=mesh['sec'=4,'blk'=8] {'blk'}, use_global_device_ids=true, to_apply=%region_13.14 | all-reduce | flops 1 | bytes 8 | tf_op jit(solution)/shard_map/psum | solution.py:54
  98.2 0.1 copy.38
  99.1 0.0 collective-permute-done
  99.1 0.1 copy.41
  99.2 10.4 %all_gather.7 = bf16[2,8,128,128]{3,2,0,1:T(8,128)(2,1)S(1)} all-gather(bf16[2,1,128,128]{3,2,0,1:T(8,128)(2,1)S(1)} %copy.41), channel_id=1, replica_groups=mesh['sec'=4,'blk'=8] {'blk'}, dimensions={1}, use_global_device_ids=true | all-gather | bytes 589824 | tf_op jit(solution)/shard_map/all_gather | solution.py:28
  109.6 1.5 multiply_reduce_fusion.3
  111.2 11.9 %psum.91 = f32[]{:T(128)} all-reduce(f32[]{:T(128)} %get-tuple-element.27), channel_id=1, replica_groups=mesh['sec'=4,'blk'=8] {'blk'}, use_global_device_ids=true, to_apply=%region_15.16 | all-reduce | flops 1 | bytes 8 | tf_op jit(solution)/shard_map/psum | solution.py:57
  123.1 2.2 %multiply_reduce_fusion.1 = (f32[]{:T(128)}, f32[]{:T(128)}, f32[8,128,1,128]{3,1,0,2:T(8,128)S(1)}) fusion(f32[8,128,1,128]{3,1,0,2:T(8,128)S(1)} %get-tuple-element.28, f32[]{:T(128)} %psum.91, f32[]{:T(128)S(6)} %sqrt.63, f32[8,128,1,128]{3,1,0,2:T(8,128)S(1)} %get-tuple-element.21, f32[128]{0:T(128)S(1)} %compare_convert_fusion, ...), kind=kOutput, calls=%fused_computation.53 | convolution fusion | flops 136577024 | bytes 2167312 | tf_op jit(solution)/shard_map/wqarc,wrbc->qarb/dot_general | solution.py:43
  125.3 13.8 %all-reduce.1 = (f32[]{:T(128)}, f32[]{:T(128)}) all-reduce(f32[]{:T(128)} %get-tuple-element.7, f32[]{:T(128)} %get-tuple-element.6), channel_id=1, replica_groups=mesh['sec'=4,'blk'=8] {'blk'}, use_global_device_ids=true, to_apply=%region_17.18 | all-reduce | flops 2 | bytes 16 | tf_op jit(solution)/shard_map/psum | solution.py:62
  142.0 1.6 multiply_reduce_fusion
  143.5 1.2 fusion.15
  144.7 12.4 %all-reduce = (f32[]{:T(128)}, f32[]{:T(128)}) all-reduce(f32[]{:T(128)} %fusion.15, f32[]{:T(128)} %get-tuple-element.18), channel_id=1, replica_groups=mesh['sec'=4,'blk'=8] {'blk'}, use_global_device_ids=true, to_apply=%region_21.22 | all-reduce | flops 2 | bytes 16 | tf_op jit(solution)/shard_map/psum | solution.py:62
  158.6 1.7 %add_multiply_fusion = f32[8,128,1,128]{3,1,0,2:T(8,128)} fusion(f32[8,128,1,128]{3,1,0,2:T(8,128)S(1)} %get-tuple-element.19, f32[]{:T(128)S(6)} %div.93, f32[]{:T(128)S(6)} %sqrt.69, f32[]{:T(128)S(6)} %div.90, f32[]{:T(128)S(6)} %sqrt.65, f32[8,128,1,128]{3,1,0,2:T(8,128)S(1)} %get-tuple-element.28, f32[]{:T(128)} %psum.91, f32[]{:T(128)S(6)} %sqrt.63, ...), kind=kLoop, calls=%fused_computation.49 | loop fusion | flops 1572864 | bytes 2101784 | tf_op jit(solution)/shard_map/mul | solution.py:107
  160.3 0.6 maximum_bitcast_fusion
  (1 shorter events, 0.0 us)
Async XLA Ops:
  0.6 30.3 %copy-start = (bf16[1,2,1,128,128]{4,3,2,1,0:T(8,128)(2,1)S(1)}, bf16[1,2,1,128,128]{4,3,2,1,0:T(8,128)(2,1)}, u32[]{:S(2)}) copy-start(bf16[1,2,1,128,128]{4,3,2,1,0:T(8,128)(2,1)} %param.9) | copy-start | bytes 196612
  0.6 0.7 copy-start.3
  0.7 0.7 copy-start.4
  2.6 0.7 copy-start.6
  3.9 0.7 copy-start.5
  4.6 14.9 %copy-start.2 = (bf16[1,2,1,128,128]{4,3,2,1,0:T(8,128)(2,1)S(1)}, bf16[1,2,1,128,128]{4,3,2,1,0:T(8,128)(2,1)}, u32[]{:S(2)}) copy-start(bf16[1,2,1,128,128]{4,3,2,1,0:T(8,128)(2,1)} %param.8) | copy-start | bytes 196612
  19.6 11.4 %copy-start.1 = (bf16[1,8,128,1,128]{4,2,3,1,0:T(8,128)(2,1)S(1)}, bf16[1,8,128,1,128]{4,2,3,1,0:T(8,128)(2,1)}, u32[]{:S(2)}) copy-start(bf16[1,8,128,1,128]{4,2,3,1,0:T(8,128)(2,1)} %param.7) | copy-start | bytes 786436
  82.3 16.7 %collective-permute-start = (bf16[2,1,128,128]{2,3,0,1:T(8,128)(2,1)S(1)}, bf16[2,1,128,128]{2,3,0,1:T(8,128)(2,1)S(1)}, u32[]{:S(2)}, u32[]{:S(2)}) collective-permute-start(bf16[2,1,128,128]{2,3,0,1:T(8,128)(2,1)S(1)} %fusion.13), channel_id=1, source_target_pairs={{0,8},{8,16},{16,24},{1,9},{9,17},{17,25},{2,10},{10,18},{18,26},{... | collective-permute-start | bytes 196616 | tf_op jit(solution)/shard_map/ppermute | solution.py:15
where the time goes:
time: 163 us; the launch traced here: 161 us
  blocking collectives  123 us (75%)
  matrix products  10.7 us (7%)
  between operations  10.7 us (7%)
  other arithmetic  10.2 us (6%)
  starting transfers between devices  3.2 us (2%)
  local copies, waits for them, and re-layouts  2.83 us (2%)
    psum x4, blocking collectives, davidson(): correlation = lax.psum(jnp.sum(residual * response), 'blk')  52.6 us
    psum x2, blocking collectives, davidson(): total = lax.psum(jnp.sum(vector * vector), 'blk')  25.1 us
    psum x2, blocking collectives, davidson(): ritz_value = lax.psum(jnp.sum(vector * image), 'blk')  23.9 us
    all_gather x2, blocking collectives, left_product(): gathered = lax.all_gather(left_block, 'blk', axis=1, tiled=True)  21.7 us
    dot_general x6, matrix products, apply_all(): jnp.einsum('wqarc,wrbc->qarb', left_done, right_block, preferred_element_...  10.2 us
    reduce_sum x2, other arithmetic, davidson(): total = lax.psum(jnp.sum(vector * vector), 'blk')  3.36 us
  transfers between devices with their start and end apart: 1, of which 0 were waited for; matrix products, arithmetic and copies ran while one was open for 0% of the time, Pallas kernels for 0%

commit v1 on v0

v1 whole, which is shorter than its diff:
```python
import functools

import jax
import jax.numpy as jnp
from jax import lax
from jax.experimental import pallas as pl
from jax.experimental.pallas import tpu as pltpu
from jax.sharding import PartitionSpec as P

MESH = pl.DeviceIdType.MESH
ITERS = 2
EPS = 1e-06
SPAN = 32.0
FLOOR = 1e-12
GROUP = 2


def partner(me, offset, count):
    if offset == 0:
        return me
    if count & (count - 1):
        return None
    result = 0
    bit = 1
    while bit < count:
        digit = lax.rem(lax.div(me, bit), 2)
        result = result + ((1 - digit) if offset & bit else digit) * bit
        bit *= 2
    return result


def target(me, offset, count):
    found = partner(me, offset, count)
    return lax.rem(me + offset, count) if found is None else found


def origin(me, offset, count):
    found = partner(me, offset, count)
    return lax.rem(me + count - offset, count) if found is None else found


def polynomial(mu, floor_squared):
    zero = jnp.zeros_like(mu[0])
    vector = [zero + 1.0]
    image = [zero, zero + 1.0]
    ritz = mu[1]
    for _ in range(ITERS):
        padded = vector + [zero]
        residual = [image[i] - ritz * padded[i] for i in range(len(image))]
        size = len(residual)
        squared = zero
        correlation = zero
        for i in range(size):
            for j in range(size):
                weight = residual[i] * residual[j]
                squared = squared + weight * mu[i + j]
                correlation = correlation + weight * mu[i + j + 1]
        squared = jnp.maximum(squared, 0.0) + floor_squared
        coupling = correlation / squared
        midpoint = 0.5 * (ritz - coupling)
        radius = jnp.sqrt(midpoint * midpoint + squared)
        cosine = jnp.sqrt(0.5 * (1.0 - midpoint / radius))
        sine = -jnp.sqrt(0.5 * (1.0 + midpoint / radius))
        tilt = sine / jnp.sqrt(squared)
        vector = [cosine * padded[i] + tilt * residual[i] for i in range(size)]
        image = [zero] + vector
        ritz = 0.5 * (ritz + coupling) - radius
    return vector, ritz


def kernel(
    count, sections, size, moments,
    left_dims, right_dims, left_labels, right_labels, guess_ref, left_ref, right_ref,
    waves_ref, energies_ref,
    guess, right, gathered, field, products, fresh, sums,
    local_sems, send_sems, recv_sems, pass_sems,
):
    sec = lax.axis_index("sec")
    me = lax.axis_index("blk")
    states = count * size
    has_next = sec < sections - 1
    has_previous = sec > 0

    load_right = pltpu.make_async_copy(right_ref, right, local_sems.at[0])
    load_left = pltpu.make_async_copy(left_ref, gathered.at[0, me], local_sems.at[1])
    load_guess = pltpu.make_async_copy(guess_ref, guess, local_sems.at[2])
    load_left.start()
    load_guess.start()
    load_right.start()

    barrier = pltpu.get_barrier_semaphore()
    for k in range(1, count):
        pl.semaphore_signal(barrier, inc=1, device_id=(sec, target(me, k, count)), device_id_type=MESH)

    @pl.when(has_next)
    def _():
        pl.semaphore_signal(barrier, inc=1, device_id=(sec + 1, me), device_id_type=MESH)

    @pl.when(has_previous)
    def _():
        pl.semaphore_signal(barrier, inc=1, device_id=(sec - 1, me), device_id_type=MESH)

    pl.semaphore_wait(barrier, count - 1 + has_next.astype(jnp.int32) + has_previous.astype(jnp.int32))

    def exchange(phase, source, slot):
        return {
            k: pltpu.make_async_remote_copy(
                src_ref=source,
                dst_ref=slot,
                send_sem=send_sems.at[phase, k],
                recv_sem=recv_sems.at[phase, k],
                device_id=(sec, target(me, k, count)),
                device_id_type=MESH,
            )
            for k in range(1, count)
        }

    first_copies = exchange(0, left_ref, gathered.at[0, me])
    for k in sorted(first_copies, reverse=True):
        first_copies[k].start()

    rows = lax.broadcasted_iota(jnp.int32, (size, size), 0)
    cols = lax.broadcasted_iota(jnp.int32, (size, size), 1)
    live_cols = cols < right_dims[0, me]
    mark = right_labels[0, me]

    def live(q):
        dims = jnp.where(left_labels[0, q] + mark == 4, left_dims[0, q], 0)
        return jnp.logical_and(rows < dims, live_cols)

    load_guess.wait()
    load_right.wait()
    right_all = right[...]
    right_peak = jnp.max(jnp.abs(right_all.astype(jnp.float32)), axis=(0, 1), keepdims=True) * SPAN

    def folded(values):
        return jnp.sum(values.reshape(-1, 8, size), axis=0)

    def chain(slot, qs, start):
        blocks = [gathered[slot, q] for q in qs]
        masks = [live(q) for q in qs]
        scales = [
            jnp.maximum(jnp.max(jnp.abs(b.astype(jnp.float32)), axis=(0, 1), keepdims=True) * right_peak, FLOOR)
            for b in blocks
        ]
        inverse = [1.0 / s for s in scales]
        powers = [[start(q, m) for q, m in zip(qs, masks)]]
        for _ in range(3):
            lefts = [
                jnp.dot(b, v.astype(jnp.bfloat16), preferred_element_type=jnp.float32).astype(jnp.bfloat16)
                for b, v in zip(blocks, powers[-1])
            ]
            lefts = [jnp.concatenate([t[:size], t[size:]], axis=1) for t in lefts]
            fulls = [jnp.dot(t, right_all, preferred_element_type=jnp.float32) for t in lefts]
            powers.append([jnp.where(m, f * i, 0.0) for m, f, i in zip(masks, fulls, inverse)])
        found = []
        for at, q in enumerate(qs):
            kept = [p[at] for p in powers]
            for i in range(3):
                field[i, q] = kept[i]
            found.append((scales[at], [folded(kept[i // 2] * kept[(i + 1) // 2]) for i in range(moments)]))
        return found

    def krylov(phase, slot, wait, start):
        found = []
        for first in range(0, count, GROUP):
            ks = range(first, min(first + GROUP, count))
            for k in ks:
                wait(k)
            found += chain(slot, [origin(me, k, count) for k in ks], start)
        peak = functools.reduce(jnp.maximum, [s for s, _ in found])
        totals = [None] * moments
        for scale, parts in found:
            ratio = scale / peak
            power = jnp.ones_like(ratio)
            for i in range(moments):
                term = parts[i] * power
                totals[i] = term if totals[i] is None else totals[i] + term
                power = power * ratio
        line = [jnp.sum(t, axis=0, keepdims=True) for t in totals]
        line.append(jnp.broadcast_to(peak, (1, size)))
        line.append(jnp.zeros((1, size), jnp.float32))
        row = phase // 2
        sums[row, me] = jnp.concatenate(line, axis=0)
        copies = exchange(phase, sums.at[row, me], sums.at[row, me])
        for k in copies:
            copies[k].start()
        for k in copies:
            copies[k].wait_recv()
        tiles = [sums[row, j] for j in range(count)]
        peaks = [t[moments : moments + 1] for t in tiles]
        top = functools.reduce(jnp.maximum, peaks)
        index = lax.broadcasted_iota(jnp.int32, (8, size), 0)
        total = jnp.zeros((8, size), jnp.float32)
        for tile, p in zip(tiles, peaks):
            ratio = p / top
            power = ratio
            weight = jnp.ones((8, size), jnp.float32)
            for i in range(1, moments):
                weight = jnp.where(index == i, power, weight)
                power = power * ratio
            total = total + tile * weight
        summed = jnp.broadcast_to(jnp.sum(total, axis=1, keepdims=True), (8, size))
        mu = [summed[i : i + 1] for i in range(moments)]
        norm = mu[0] + EPS
        mu = [m / norm for m in mu]
        relative = EPS**0.5 / top
        vector, ritz = polynomial(mu, relative * relative)
        shrink = lax.rsqrt(norm)
        weights = {}
        for k, (scale, _) in enumerate(found):
            ratio = scale / top
            weights[k] = [vector[0] * shrink, vector[1] * shrink * ratio, vector[2] * shrink * ratio * ratio]
        return weights, ritz * top, copies

    def combined(q, weight):
        return weight[0] * field[0, q] + weight[1] * field[1, q] + weight[2] * field[2, q]

    def wait_first(k):
        if k == 0:
            load_left.wait()
        else:
            first_copies[k].wait_recv()

    weights, first_ritz, first_sums = krylov(
        1, 0, wait_first, lambda q, m: jnp.where(m, guess[q].astype(jnp.float32), 0.0)
    )

    total = jnp.zeros((size, 2 * size), jnp.float32)
    for k in range(count):
        q = origin(me, k, count)
        vector = combined(q, weights[k])
        field[0, q] = vector
        rounded = vector.astype(jnp.bfloat16)
        done = jnp.dot(gathered[0, q], rounded, preferred_element_type=jnp.float32).astype(jnp.bfloat16)
        done = jnp.concatenate([done[:size], done[size:]], axis=1)
        total = total + lax.dot_general(
            rounded, done, (((0,), (0,)), ((), ())), preferred_element_type=jnp.float32
        )
    total = (states * total).astype(jnp.bfloat16)
    fresh[:size] = total[:, :size]
    fresh[size:] = total[:, size:]

    onward = pltpu.make_async_remote_copy(
        src_ref=fresh,
        dst_ref=gathered.at[1, me],
        send_sem=pass_sems.at[0],
        recv_sem=pass_sems.at[1],
        device_id=(lax.rem(sec + 1, sections), me),
        device_id_type=MESH,
    )

    @pl.when(has_next)
    def _():
        onward.start()

    second_copies = exchange(2, gathered.at[1, me], gathered.at[1, me])

    @pl.when(has_previous)
    def _():
        onward.wait_recv()
        for k in sorted(second_copies, reverse=True):
            second_copies[k].start()

    def wait_second(k):
        if k:

            @pl.when(has_previous)
            def _():
                second_copies[k].wait_recv()

    slot = jnp.where(has_previous, 1, 0)
    weights, second_ritz, second_sums = krylov(3, slot, wait_second, lambda q, m: field[0, q])

    for k in range(count):
        q = origin(me, k, count)
        waves_ref[q] = states * combined(q, weights[k])
    lane = lax.broadcasted_iota(jnp.int32, (1, size), 1)
    energies_ref[...] = jnp.where(lane == 0, first_ritz, second_ritz)[:, :2]

    for copies in (first_copies, first_sums, second_sums):
        for k in copies:
            copies[k].wait_send()

    @pl.when(has_previous)
    def _():
        for k in second_copies:
            second_copies[k].wait_send()

    @pl.when(has_next)
    def _():
        onward.wait_send()


def solution(mesh):
    count = mesh.shape["blk"]
    sections = mesh.shape["sec"]

    def local(guess, left_env, right_env, left_dims, right_dims, left_labels, right_labels):
        size = guess.shape[2]
        terms = left_env.shape[1]
        rows = terms * size
        smem = pl.BlockSpec(memory_space=pltpu.SMEM)
        anywhere = pl.BlockSpec(memory_space=pl.ANY)
        vmem = pl.BlockSpec(memory_space=pltpu.VMEM)
        moments = 2 * ITERS + 2
        waves, energies = pl.pallas_call(
            functools.partial(kernel, count, sections, size, moments),
            out_shape=(
                jax.ShapeDtypeStruct((count, size, size), jnp.float32),
                jax.ShapeDtypeStruct((1, 2), jnp.float32),
            ),
            in_specs=[smem] * 4 + [anywhere] * 3,
            out_specs=(vmem, vmem),
            scratch_shapes=[
                pltpu.VMEM((count, size, size), jnp.bfloat16),
                pltpu.VMEM((rows, size), jnp.bfloat16),
                pltpu.VMEM((2, count, rows, size), jnp.bfloat16),
                pltpu.VMEM((3, count, size, size), jnp.float32),
                pltpu.VMEM((8, size), jnp.float32),
                pltpu.VMEM((rows, size), jnp.bfloat16),
                pltpu.VMEM((2, count, 8, size), jnp.float32),
                pltpu.SemaphoreType.DMA((3,)),
                pltpu.SemaphoreType.DMA((4, count)),
                pltpu.SemaphoreType.DMA((4, count)),
                pltpu.SemaphoreType.DMA((2,)),
            ],
            compiler_params=pltpu.CompilerParams(
                collective_id=0, has_side_effects=True, vmem_limit_bytes=40 * 1024 * 1024
            ),
        )(
            left_dims, right_dims, left_labels, right_labels,
            guess.reshape(count, size, size), left_env.reshape(rows, size), right_env.reshape(rows, size),
        )
        return waves.reshape(1, count, size, 1, size), energies

    return jax.shard_map(
        local,
        mesh=mesh,
        in_specs=(
            P("sec", None, None, "blk", None),
            P("sec", None, "blk", None, None),
            P("sec", None, "blk", None, None),
            P("sec", None),
            P("sec", None),
            P("sec", None),
            P("sec", None),
        ),
        out_specs=(P("sec", None, None, "blk", None), P("sec", None)),
        check_vma=False,
    )
```

time: 163 us -> 40.6 us (0.25); the launches traced: 161 us -> 40.3 us
  blocking collectives: 123 us -> 0 us
  Pallas kernels: 0 us -> 35 us
  matrix products: 10.7 us -> 0 us
  other arithmetic: 10.2 us -> 0 us
  between operations: 10.7 us -> 0.68 us
  starting transfers between devices: 3.2 us -> 0 us
  local copies, waits for them, and re-layouts: 2.83 us -> 4.6 us
    psum x8 -> x0, blocking collectives: 102 us -> none  [the longest x4 52.6 us: davidson(): correlation = lax.psum(jnp.sum(residual * response), 'blk')]
    pallas_call x0 -> x1, Pallas kernels: none -> 35 us  [local(): pl.pallas_call(functools.partial(kernel, count, sections, size, moments),...]
    all_gather x2 -> x0, blocking collectives: 21.7 us -> none  [left_product(): gathered = lax.all_gather(left_block, 'blk', axis=1, tiled=True)]
    dot_general x7 -> x0, matrix products: 10.7 us -> none  [the longest x6 10.2 us: apply_all(): jnp.einsum('wqarc,wrbc->qarb', left_done, right_block, preferred_element_...]
    reduce_sum x4 -> x0, other arithmetic: 6.49 us -> none  [the longest x2 3.36 us: davidson(): total = lax.psum(jnp.sum(vector * vector), 'blk')]
    ppermute x1 -> x0, starting transfers between devices: 3.2 us -> none  [from_behind(): return lax.ppermute(block, axis, route)]
    unnamed x15 -> x16, local copies, waits for them, and re-layouts: 2.12 us -> 4.6 us
    mul x2 -> x0, other arithmetic: 1.79 us -> none  [the longest x1 1.72 us: local(): waves = (states * second_vector)[None]]
  transfers between devices with their start and end apart: 1 -> 0, of which waited for: 0 -> 0; matrix products, arithmetic and copies ran while one was open for 0% -> 0% of each run, Pallas kernels for 0% -> 0%
where the time goes in v1:
time: 40.6 us; the launch traced here: 40.3 us
  Pallas kernels  35 us (86%)
  local copies, waits for them, and re-layouts  4.6 us (11%)
  between operations  0.68 us (2%)
    pallas_call x1, Pallas kernels, local(): pl.pallas_call(functools.partial(kernel, count, sections, size, moments),...  35 us
    unnamed x16, local copies, waits for them, and re-layouts  4.6 us

profile of v1, /device:TPU:9, one launch (start us, length us, event | category | flops | bytes accessed | tf_op | source)
XLA Modules:
  0.0 40.3 jit_solution(13477525126970837645)
XLA Ops:
  0.6 0.0 copy-start.6
  0.6 0.0 copy-start.3
  0.7 0.0 copy-start.4
  0.7 0.0 copy-start.5
  0.7 0.6 %copy-done.6 = s32[1,8]{1,0:T(1,128)S(1)} copy-done((s32[1,8]{1,0:T(1,128)S(1)}, s32[1,8]{1,0:T(1,128)}, u32[]{:S(2)}) %copy-start.6) | copy-done | bytes 56
  1.3 0.0 copy-done.3
  1.3 0.0 copy-done.4
  1.3 0.0 copy-done.5
  1.3 0.0 copy-start
  1.3 0.9 %copy-done = bf16[1,8,128,1,128]{4,2,3,1,0:T(8,128)(2,1)S(1)} copy-done((bf16[1,8,128,1,128]{4,2,3,1,0:T(8,128)(2,1)S(1)}, bf16[1,8,128,1,128]{4,2,3,1,0:T(8,128)(2,1)}, u32[]{:S(2)}) %copy-start) | copy-done | bytes 262168
  2.3 0.0 copy-start.1
  2.3 0.8 %copy-done.1 = bf16[1,2,1,128,128]{4,3,2,1,0:T(8,128)(2,1)S(1)} copy-done((bf16[1,2,1,128,128]{4,3,2,1,0:T(8,128)(2,1)S(1)}, bf16[1,2,1,128,128]{4,3,2,1,0:T(8,128)(2,1)}, u32[]{:S(2)}) %copy-start.1) | copy-done | bytes 65560
  3.1 0.0 copy-start.2
  3.1 0.8 %copy-done.2 = bf16[1,2,1,128,128]{4,3,2,1,0:T(8,128)(2,1)S(1)} copy-done((bf16[1,2,1,128,128]{4,3,2,1,0:T(8,128)(2,1)S(1)}, bf16[1,2,1,128,128]{4,3,2,1,0:T(8,128)(2,1)}, u32[]{:S(2)}) %copy-start.2) | copy-done | bytes 65560
  4.0 35.0 %shard_map.86 = (f32[8,128,128]{2,1,0:T(8,128)S(1)}, f32[1,2]{1,0:T(1,128)S(1)}) custom-call(s32[1,8]{1,0:T(1,128)S(1)} %copy-done.3, s32[1,8]{1,0:T(1,128)S(1)} %copy-done.4, s32[1,8]{1,0:T(1,128)S(1)} %copy-done.5, s32[1,8]{1,0:T(1,128)S(1)} %copy-done.6, bf16[8,128,128]{2,1,0:T(8,128)(2,1)S(1)} %bitcast.7, bf16[256,128]{1,0:T(8,128)(2,1)S(1)} %bitcast.8, ...), custom_call_target="tpu_custom_call" | custom-call | tf_op jit(solution)/shard_map/pallas_call | solution.py:307
  39.0 0.8 %copy.12 = f32[1,8,128,1,128]{4,3,2,1,0:T(1,128)} copy(f32[1,8,128,1,128]{4,3,2,1,0:T(1,128)S(1)} %bitcast.6) | data formatting | bytes 1048576
  39.8 0.5 %copy.13 = f32[1,2]{1,0:T(1,128)} copy(f32[1,2]{1,0:T(1,128)S(1)} %get-tuple-element.11) | data formatting | bytes 16
Async XLA Ops:
  0.6 0.7 %copy-start.6 = (s32[1,8]{1,0:T(1,128)S(1)}, s32[1,8]{1,0:T(1,128)}, u32[]{:S(2)}) copy-start(s32[1,8]{1,0:T(1,128)} %right_labels.1) | copy-start | bytes 100
  0.6 0.7 %copy-start.3 = (s32[1,8]{1,0:T(1,128)S(1)}, s32[1,8]{1,0:T(1,128)}, u32[]{:S(2)}) copy-start(s32[1,8]{1,0:T(1,128)} %left_dims.1) | copy-start | bytes 100
  0.7 0.7 %copy-start.4 = (s32[1,8]{1,0:T(1,128)S(1)}, s32[1,8]{1,0:T(1,128)}, u32[]{:S(2)}) copy-start(s32[1,8]{1,0:T(1,128)} %right_dims.1) | copy-start | bytes 100
  0.7 0.7 %copy-start.5 = (s32[1,8]{1,0:T(1,128)S(1)}, s32[1,8]{1,0:T(1,128)}, u32[]{:S(2)}) copy-start(s32[1,8]{1,0:T(1,128)} %left_labels.1) | copy-start | bytes 100
  1.3 0.9 %copy-start = (bf16[1,8,128,1,128]{4,2,3,1,0:T(8,128)(2,1)S(1)}, bf16[1,8,128,1,128]{4,2,3,1,0:T(8,128)(2,1)}, u32[]{:S(2)}) copy-start(bf16[1,8,128,1,128]{4,2,3,1,0:T(8,128)(2,1)} %param.7) | copy-start | bytes 786436
  2.3 0.8 %copy-start.1 = (bf16[1,2,1,128,128]{4,3,2,1,0:T(8,128)(2,1)S(1)}, bf16[1,2,1,128,128]{4,3,2,1,0:T(8,128)(2,1)}, u32[]{:S(2)}) copy-start(bf16[1,2,1,128,128]{4,3,2,1,0:T(8,128)(2,1)} %param.8) | copy-start | bytes 196612
  3.1 0.8 %copy-start.2 = (bf16[1,2,1,128,128]{4,3,2,1,0:T(8,128)(2,1)S(1)}, bf16[1,2,1,128,128]{4,3,2,1,0:T(8,128)(2,1)}, u32[]{:S(2)}) copy-start(bf16[1,2,1,128,128]{4,3,2,1,0:T(8,128)(2,1)} %param.9) | copy-start | bytes 196612

commit v2 on v1

v2 whole, which is shorter than its diff:
```python
import functools

import jax
import jax.numpy as jnp
from jax import lax
from jax.experimental import pallas as pl
from jax.experimental.pallas import tpu as pltpu
from jax.sharding import PartitionSpec as P

MESH = pl.DeviceIdType.MESH
ITERS = 2
EPS = 1e-06
SPAN = 32.0
FLOOR = 1e-12
GROUP = 4
TOTAL = 4


def target(me, offset, count):
    chip = lax.rem(lax.div(me, 2) + offset // 2, count // 2)
    return chip * 2 + lax.rem(me + offset, 2)


def origin(me, offset, count):
    chip = lax.rem(lax.div(me, 2) + count // 2 - offset // 2, count // 2)
    return chip * 2 + lax.rem(me + offset, 2)


def polynomial(mu, floor_squared):
    zero = jnp.zeros_like(mu[0])
    vector = [zero + 1.0]
    image = [zero, zero + 1.0]
    ritz = mu[1]
    for _ in range(ITERS):
        padded = vector + [zero]
        residual = [image[i] - ritz * padded[i] for i in range(len(image))]
        size = len(residual)
        squared = zero
        correlation = zero
        for i in range(size):
            for j in range(size):
                weight = residual[i] * residual[j]
                squared = squared + weight * mu[i + j]
                correlation = correlation + weight * mu[i + j + 1]
        squared = jnp.maximum(squared, 0.0) + floor_squared
        coupling = correlation / squared
        midpoint = 0.5 * (ritz - coupling)
        radius = jnp.sqrt(midpoint * midpoint + squared)
        cosine = jnp.sqrt(0.5 * (1.0 - midpoint / radius))
        sine = -jnp.sqrt(0.5 * (1.0 + midpoint / radius))
        tilt = sine / jnp.sqrt(squared)
        vector = [cosine * padded[i] + tilt * residual[i] for i in range(size)]
        image = [zero] + vector
        ritz = 0.5 * (ritz + coupling) - radius
    return vector, ritz


def kernel(
    count, sections, size, moments,
    left_dims, right_dims, left_labels, right_labels, guess_ref, left_ref, right_ref,
    waves_ref, energies_ref,
    guess, right, first_env, second_env, field, stats, fresh, sums, owner,
    local_sems, send_sems, recv_sems, pass_sems,
):
    sec = lax.axis_index("sec")
    me = lax.axis_index("blk")
    states = count * size
    slots = count - TOTAL
    has_next = sec < sections - 1
    has_previous = sec > 0

    load_left = pltpu.make_async_copy(left_ref, first_env.at[me], local_sems.at[1])
    load_guess = pltpu.make_async_copy(guess_ref, guess, local_sems.at[2])
    load_right = pltpu.make_async_copy(right_ref, right, local_sems.at[0])
    load_left.start()
    load_guess.start()
    load_right.start()

    barrier = pltpu.get_barrier_semaphore()
    for k in range(1, count):
        pl.semaphore_signal(barrier, inc=1, device_id=(sec, target(me, k, count)), device_id_type=MESH)

    @pl.when(has_next)
    def _():
        pl.semaphore_signal(barrier, inc=1, device_id=(sec + 1, me), device_id_type=MESH)

    @pl.when(has_previous)
    def _():
        pl.semaphore_signal(barrier, inc=1, device_id=(sec - 1, me), device_id_type=MESH)

    mark = right_labels[0, me]
    places = []
    seen = jnp.int32(0)
    matches = []
    for q in range(count):
        match = left_labels[0, q] + mark == TOTAL
        places.append(seen)
        matches.append(match)
        seen = seen + match.astype(jnp.int32)
    for t in range(slots):
        sector = jnp.int32(0)
        dims = jnp.int32(0)
        for q in range(count):
            here = jnp.logical_and(matches[q], places[q] == t)
            sector = jnp.where(here, q, sector)
            dims = jnp.where(here, left_dims[0, q], dims)
        owner[0, t] = sector
        owner[1, t] = dims

    load_left.wait()
    pl.semaphore_wait(barrier, count - 1 + has_next.astype(jnp.int32) + has_previous.astype(jnp.int32))

    def copy_to(phase, k, hop, source, slot):
        return pltpu.make_async_remote_copy(
            src_ref=source,
            dst_ref=slot,
            send_sem=send_sems.at[phase, k],
            recv_sem=recv_sems.at[phase, k],
            device_id=(sec, target(me, hop, count)),
            device_id_type=MESH,
        )

    def gather(phase, env):
        copies = {}
        for k in list(range(2, count, 2)) + [1]:
            copies[k] = copy_to(phase, k, k, env.at[me], env.at[me])
            copies[k].start()
        for k in range(2, count, 2):
            block = env.at[origin(me, k, count)]
            copies[k].wait_recv()
            copies[k + 1] = copy_to(phase, k + 1, 1, block, block)
            copies[k + 1].start()
        for k in range(1, count, 2):
            copies[k].wait_recv()
        for k in copies:
            copies[k].wait_send()

    gather(0, first_env)

    @pl.when(jnp.logical_not(has_previous))
    def _():
        pltpu.make_async_copy(first_env, second_env, local_sems.at[3]).start()

    rows = lax.broadcasted_iota(jnp.int32, (size, size), 0)
    cols = lax.broadcasted_iota(jnp.int32, (size, size), 1)
    live_cols = cols < right_dims[0, me]

    load_guess.wait()
    load_right.wait()
    right_all = right[...]
    right_peak = jnp.max(jnp.abs(right_all.astype(jnp.float32)), axis=(0, 1), keepdims=True) * SPAN

    def folded(values):
        return jnp.sum(values.reshape(-1, 8, size), axis=0)

    def chain(env, ts, start):
        sectors = [owner[0, t] for t in ts]
        blocks = [env[q] for q in sectors]
        masks = [jnp.logical_and(rows < owner[1, t], live_cols) for t in ts]
        scales = [
            jnp.maximum(jnp.max(jnp.abs(b.astype(jnp.float32)), axis=(0, 1), keepdims=True) * right_peak, FLOOR)
            for b in blocks
        ]
        inverse = [1.0 / s for s in scales]
        powers = [[start(t, q, m) for t, q, m in zip(ts, sectors, masks)]]
        for _ in range(3):
            lefts = [
                jnp.dot(b, v.astype(jnp.bfloat16), preferred_element_type=jnp.float32).astype(jnp.bfloat16)
                for b, v in zip(blocks, powers[-1])
            ]
            lefts = [jnp.concatenate([x[:size], x[size:]], axis=1) for x in lefts]
            full = jnp.dot(jnp.concatenate(lefts, axis=0), right_all, preferred_element_type=jnp.float32)
            powers.append([
                jnp.where(m, full[at * size : (at + 1) * size] * i, 0.0)
                for at, (m, i) in enumerate(zip(masks, inverse))
            ])
        for at, t in enumerate(ts):
            kept = [p[at] for p in powers]
            for i in range(3):
                field[i, t] = kept[i]
            line = [
                jnp.sum(folded(kept[i // 2] * kept[(i + 1) // 2]), axis=0, keepdims=True) for i in range(moments)
            ]
            line.append(jnp.broadcast_to(scales[at], (1, size)))
            line.append(jnp.zeros((1, size), jnp.float32))
            stats[t] = jnp.concatenate(line, axis=0)

    index = lax.broadcasted_iota(jnp.int32, (8, size), 0)

    def merged(tiles):
        peaks = [tile[moments : moments + 1] for tile in tiles]
        top = functools.reduce(jnp.maximum, peaks)
        total = jnp.zeros((8, size), jnp.float32)
        for tile, peak in zip(tiles, peaks):
            ratio = peak / top
            power = ratio
            weight = jnp.ones((8, size), jnp.float32)
            for i in range(1, moments):
                weight = jnp.where(index == i, power, weight)
                power = power * ratio
            total = total + tile * weight
        return jnp.where(index == moments, top, total), top

    def krylov(phase, env, start):
        if slots % GROUP == 0 and slots > GROUP:

            def step(g, carry):
                chain(env, [g * GROUP + i for i in range(GROUP)], start)
                return carry

            lax.fori_loop(0, slots // GROUP, step, 0)
        else:
            for first in range(0, slots, GROUP):
                chain(env, list(range(first, min(first + GROUP, slots))), start)
        row = phase // 2
        tiles = [stats[t] for t in range(slots)]
        sums[row, me] = merged(tiles)[0]
        copies = {k: copy_to(phase, k, k, sums.at[row, me], sums.at[row, me]) for k in range(1, count)}
        for k in copies:
            copies[k].start()
        for k in copies:
            copies[k].wait_recv()
        total, top = merged([sums[row, j] for j in range(count)])
        summed = jnp.broadcast_to(jnp.sum(total, axis=1, keepdims=True), (8, size))
        mu = [summed[i : i + 1] for i in range(moments)]
        norm = mu[0] + EPS
        mu = [m / norm for m in mu]
        relative = EPS**0.5 / top
        vector, ritz = polynomial(mu, relative * relative)
        shrink = lax.rsqrt(norm)
        weights = []
        for tile in tiles:
            ratio = tile[moments : moments + 1] / top
            weights.append([vector[0] * shrink, vector[1] * shrink * ratio, vector[2] * shrink * ratio * ratio])
        return weights, ritz * top, copies

    def combined(t, weight):
        return weight[0] * field[0, t] + weight[1] * field[1, t] + weight[2] * field[2, t]

    weights, first_ritz, first_sums = krylov(
        1, first_env, lambda t, q, m: jnp.where(m, guess[q].astype(jnp.float32), 0.0)
    )

    total = jnp.zeros((size, 2 * size), jnp.float32)
    for t in range(slots):
        vector = combined(t, weights[t])
        field[0, t] = vector
        rounded = vector.astype(jnp.bfloat16)
        done = jnp.dot(first_env[owner[0, t]], rounded, preferred_element_type=jnp.float32).astype(jnp.bfloat16)
        done = jnp.concatenate([done[:size], done[size:]], axis=1)
        total = total + lax.dot_general(
            rounded, done, (((0,), (0,)), ((), ())), preferred_element_type=jnp.float32
        )
    total = (states * total).astype(jnp.bfloat16)
    fresh[:size] = total[:, :size]
    fresh[size:] = total[:, size:]

    onward = pltpu.make_async_remote_copy(
        src_ref=fresh,
        dst_ref=second_env.at[me],
        send_sem=pass_sems.at[0],
        recv_sem=pass_sems.at[1],
        device_id=(lax.rem(sec + 1, sections), me),
        device_id_type=MESH,
    )

    @pl.when(has_next)
    def _():
        onward.start()

    @pl.when(has_previous)
    def _():
        onward.wait_recv()
        gather(2, second_env)

    @pl.when(jnp.logical_not(has_previous))
    def _():
        pltpu.make_async_copy(first_env, second_env, local_sems.at[3]).wait()

    weights, second_ritz, second_sums = krylov(3, second_env, lambda t, q, m: field[0, t])

    for t in range(slots):
        field[0, t] = states * combined(t, weights[t])
    for q in range(count):
        waves_ref[q] = jnp.where(matches[q], field[0, jnp.minimum(places[q], slots - 1)], 0.0)
    lane = lax.broadcasted_iota(jnp.int32, (1, size), 1)
    energies_ref[...] = jnp.where(lane == 0, first_ritz, second_ritz)[:, :2]

    for copies in (first_sums, second_sums):
        for k in copies:
            copies[k].wait_send()

    @pl.when(has_next)
    def _():
        onward.wait_send()


def solution(mesh):
    count = mesh.shape["blk"]
    sections = mesh.shape["sec"]

    def local(guess, left_env, right_env, left_dims, right_dims, left_labels, right_labels):
        size = guess.shape[2]
        terms = left_env.shape[1]
        rows = terms * size
        smem = pl.BlockSpec(memory_space=pltpu.SMEM)
        anywhere = pl.BlockSpec(memory_space=pltpu.HBM)
        vmem = pl.BlockSpec(memory_space=pltpu.VMEM)
        moments = 2 * ITERS + 2
        waves, energies = pl.pallas_call(
            functools.partial(kernel, count, sections, size, moments),
            out_shape=(
                jax.ShapeDtypeStruct((count, size, size), jnp.float32),
                jax.ShapeDtypeStruct((1, 2), jnp.float32),
            ),
            in_specs=[smem] * 4 + [anywhere] * 3,
            out_specs=(vmem, vmem),
            scratch_shapes=[
                pltpu.VMEM((count, size, size), jnp.bfloat16),
                pltpu.VMEM((rows, size), jnp.bfloat16),
                pltpu.VMEM((count, rows, size), jnp.bfloat16),
                pltpu.VMEM((count, rows, size), jnp.bfloat16),
                pltpu.VMEM((3, count - TOTAL, size, size), jnp.float32),
                pltpu.VMEM((count - TOTAL, 8, size), jnp.float32),
                pltpu.VMEM((rows, size), jnp.bfloat16),
                pltpu.VMEM((2, count, 8, size), jnp.float32),
                pltpu.SMEM((2, count), jnp.int32),
                pltpu.SemaphoreType.DMA((4,)),
                pltpu.SemaphoreType.DMA((4, count)),
                pltpu.SemaphoreType.DMA((4, count)),
                pltpu.SemaphoreType.DMA((2,)),
            ],
            compiler_params=pltpu.CompilerParams(
                collective_id=0, has_side_effects=True, vmem_limit_bytes=64800 * 1024
            ),
        )(
            left_dims, right_dims, left_labels, right_labels,
            guess.reshape(count, size, size), left_env.reshape(rows, size), right_env.reshape(rows, size),
        )
        return waves.reshape(1, count, size, 1, size), energies

    return jax.shard_map(
        local,
        mesh=mesh,
        in_specs=(
            P("sec", None, None, "blk", None),
            P("sec", None, "blk", None, None),
            P("sec", None, "blk", None, None),
            P("sec", None),
            P("sec", None),
            P("sec", None),
            P("sec", None),
        ),
        out_specs=(P("sec", None, None, "blk", None), P("sec", None)),
        check_vma=False,
    )
```

time: 40.6 us -> 31.9 us (0.79)
  Pallas kernels: 35 us -> 28.7 us
  local copies, waits for them, and re-layouts: 4.6 us -> 2.39 us
    pallas_call x1, Pallas kernels: 35 us -> 28.7 us  [local(): pl.pallas_call(functools.partial(kernel, count, sections, size, moments),...]
    unnamed x16 -> x4, local copies, waits for them, and re-layouts: 4.6 us -> 2.39 us
where the time goes in v2:
time: 31.9 us; the launch traced here: 31.8 us
  Pallas kernels  28.7 us (90%)
  local copies, waits for them, and re-layouts  2.39 us (7%)
  between operations  0.65 us (2%)
    pallas_call x1, Pallas kernels, local(): pl.pallas_call(functools.partial(kernel, count, sections, size, moments),...  28.7 us
    unnamed x4, local copies, waits for them, and re-layouts  2.39 us

profile of v2, /device:TPU:9, one launch (start us, length us, event | category | flops | bytes accessed | tf_op | source)
XLA Modules:
  0.0 31.8 jit_solution(7554576993067804010)
XLA Ops:
  0.6 28.7 %shard_map.86 = (f32[8,128,128]{2,1,0:T(8,128)}, f32[1,2]{1,0:T(1,128)}) custom-call(s32[1,8]{1,0:T(1,128)} %left_dims.1, s32[1,8]{1,0:T(1,128)} %right_dims.1, s32[1,8]{1,0:T(1,128)} %left_labels.1, s32[1,8]{1,0:T(1,128)} %right_labels.1, bf16[8,128,128]{2,1,0:T(8,128)(2,1)} %bitcast.7, bf16[256,128]{1,0:T(8,128)(2,1)} %bitcast.8, bf16[256,128]{1,0:T(8,128)(2,1)} %bitcast.9), custom_call_target="tpu_custom_call" | custom-call | tf_op jit(solution)/shard_map/pallas_call | solution.py:310
  29.4 0.0 copy-start
  29.4 1.9 %copy.12 = f32[1,8,128,1,128]{4,3,2,1,0:T(1,128)} copy(f32[1,8,128,1,128]{4,3,2,1,0:T(1,128)} %bitcast.6) | data formatting | bytes 1048576
  31.2 0.0 copy-done
  31.2 0.5 %copy.13 = f32[1,2]{1,0:T(1,128)} copy(f32[1,2]{1,0:T(1,128)S(1)} %copy-done) | data formatting | bytes 16
Async XLA Ops:
  29.4 1.9 %copy-start = (f32[1,2]{1,0:T(1,128)S(1)}, f32[1,2]{1,0:T(1,128)}, u32[]{:S(2)}) copy-start(f32[1,2]{1,0:T(1,128)} %get-tuple-element.11) | copy-start | bytes 28

commit v3 on v2

--- a/solution.py
+++ b/solution.py
@@ -14,6 +14,7 @@
 FLOOR = 1e-12
 GROUP = 4
 TOTAL = 4
+TERMS = 2
 
 
 def target(me, offset, count):
@@ -110,32 +111,40 @@
     load_left.wait()
     pl.semaphore_wait(barrier, count - 1 + has_next.astype(jnp.int32) + has_previous.astype(jnp.int32))
 
-    def copy_to(phase, k, hop, source, slot):
+    def copy_to(phase, k, hop, source, slot, part=0):
         return pltpu.make_async_remote_copy(
             src_ref=source,
             dst_ref=slot,
-            send_sem=send_sems.at[phase, k],
-            recv_sem=recv_sems.at[phase, k],
+            send_sem=send_sems.at[phase, k, part],
+            recv_sem=recv_sems.at[phase, k, part],
             device_id=(sec, target(me, hop, count)),
             device_id_type=MESH,
         )
 
-    def gather(phase, env):
+    def term(ref, w):
+        return ref.at[pl.ds(w * size, size)]
+
+    def gather(phase, env, arrive):
         copies = {}
-        for k in list(range(2, count, 2)) + [1]:
-            copies[k] = copy_to(phase, k, k, env.at[me], env.at[me])
-            copies[k].start()
-        for k in range(2, count, 2):
-            block = env.at[origin(me, k, count)]
-            copies[k].wait_recv()
-            copies[k + 1] = copy_to(phase, k + 1, 1, block, block)
-            copies[k + 1].start()
-        for k in range(1, count, 2):
-            copies[k].wait_recv()
-        for k in copies:
-            copies[k].wait_send()
-
-    gather(0, first_env)
+        for w in range(TERMS):
+            arrive(w)
+            block = term(env.at[me], w)
+            for k in list(range(2, count, 2)) + [1]:
+                copies[k, w] = copy_to(phase, k, k, block, block, w)
+                copies[k, w].start()
+        for w in range(TERMS):
+            for k in range(2, count, 2):
+                block = term(env.at[origin(me, k, count)], w)
+                copies[k, w].wait_recv()
+                copies[k + 1, w] = copy_to(phase, k + 1, 1, block, block, w)
+                copies[k + 1, w].start()
+        for w in range(TERMS):
+            for k in range(1, count, 2):
+                copies[k, w].wait_recv()
+        for key in copies:
+            copies[key].wait_send()
+
+    gather(0, first_env, lambda w: None)
 
     @pl.when(jnp.logical_not(has_previous))
     def _():
@@ -241,37 +250,39 @@
         1, first_env, lambda t, q, m: jnp.where(m, guess[q].astype(jnp.float32), 0.0)
     )
 
-    total = jnp.zeros((size, 2 * size), jnp.float32)
+    onward = [
+        pltpu.make_async_remote_copy(
+            src_ref=term(fresh, w),
+            dst_ref=term(second_env.at[me], w),
+            send_sem=pass_sems.at[0, w],
+            recv_sem=pass_sems.at[1, w],
+            device_id=(lax.rem(sec + 1, sections), me),
+            device_id_type=MESH,
+        )
+        for w in range(TERMS)
+    ]
+    rounded = []
     for t in range(slots):
         vector = combined(t, weights[t])
         field[0, t] = vector
-        rounded = vector.astype(jnp.bfloat16)
-        done = jnp.dot(first_env[owner[0, t]], rounded, preferred_element_type=jnp.float32).astype(jnp.bfloat16)
-        done = jnp.concatenate([done[:size], done[size:]], axis=1)
-        total = total + lax.dot_general(
-            rounded, done, (((0,), (0,)), ((), ())), preferred_element_type=jnp.float32
-        )
-    total = (states * total).astype(jnp.bfloat16)
-    fresh[:size] = total[:, :size]
-    fresh[size:] = total[:, size:]
-
-    onward = pltpu.make_async_remote_copy(
-        src_ref=fresh,
-        dst_ref=second_env.at[me],
-        send_sem=pass_sems.at[0],
-        recv_sem=pass_sems.at[1],
-        device_id=(lax.rem(sec + 1, sections), me),
-        device_id_type=MESH,
-    )
-
-    @pl.when(has_next)
-    def _():
-        onward.start()
+        rounded.append(vector.astype(jnp.bfloat16))
+    for w in range(TERMS):
+        total = jnp.zeros((size, size), jnp.float32)
+        for t in range(slots):
+            block = first_env[owner[0, t], w * size : (w + 1) * size]
+            done = jnp.dot(block, rounded[t], preferred_element_type=jnp.float32).astype(jnp.bfloat16)
+            total = total + lax.dot_general(
+                rounded[t], done, (((0,), (0,)), ((), ())), preferred_element_type=jnp.float32
+            )
+        fresh[w * size : (w + 1) * size] = (states * total).astype(jnp.bfloat16)
+
+        @pl.when(has_next)
+        def _(w=w):
+            onward[w].start()
 
     @pl.when(has_previous)
     def _():
-        onward.wait_recv()
-        gather(2, second_env)
+        gather(2, second_env, lambda w: onward[w].wait_recv())
 
     @pl.when(jnp.logical_not(has_previous))
     def _():
@@ -292,7 +303,8 @@
 
     @pl.when(has_next)
     def _():
-        onward.wait_send()
+        for copy in onward:
+            copy.wait_send()
 
 
 def solution(mesh):
@@ -310,8 +322,8 @@
         waves, energies = pl.pallas_call(
             functools.partial(kernel, count, sections, size, moments),
             out_shape=(
-                jax.ShapeDtypeStruct((count, size, size), jnp.float32),
-                jax.ShapeDtypeStruct((1, 2), jnp.float32),
+                pltpu.VMEM((count, size, size), jnp.float32),
+                pltpu.VMEM((1, 2), jnp.float32),
             ),
             in_specs=[smem] * 4 + [anywhere] * 3,
             out_specs=(vmem, vmem),
@@ -326,12 +338,12 @@
                 pltpu.VMEM((2, count, 8, size), jnp.float32),
                 pltpu.SMEM((2, count), jnp.int32),
                 pltpu.SemaphoreType.DMA((4,)),
-                pltpu.SemaphoreType.DMA((4, count)),
-                pltpu.SemaphoreType.DMA((4, count)),
-                pltpu.SemaphoreType.DMA((2,)),
+                pltpu.SemaphoreType.DMA((4, count, TERMS)),
+                pltpu.SemaphoreType.DMA((4, count, TERMS)),
+                pltpu.SemaphoreType.DMA((2, TERMS)),
             ],
             compiler_params=pltpu.CompilerParams(
-                collective_id=0, has_side_effects=True, vmem_limit_bytes=64800 * 1024
+                collective_id=0, has_side_effects=True, vmem_limit_bytes=64 * 1024 * 1024 - 10 * count * size * size
             ),
         )(
             left_dims, right_dims, left_labels, right_labels,

time: 31.9 us -> 30.1 us (0.944)
  local copies, waits for them, and re-layouts: 2.39 us -> 1.31 us
  Pallas kernels: 28.7 us -> 27.9 us
    unnamed x4 -> x2, local copies, waits for them, and re-layouts: 2.39 us -> 1.31 us
    pallas_call x1, Pallas kernels: 28.7 us -> 27.9 us  [local(): pl.pallas_call(functools.partial(kernel, count, sections, size, moments),...]
where the time goes in v3:
time: 30.1 us; the launch traced here: 29.9 us
  Pallas kernels  27.9 us (93%)
  local copies, waits for them, and re-layouts  1.31 us (4%)
  between operations  0.64 us (2%)
    pallas_call x1, Pallas kernels, local(): pl.pallas_call(functools.partial(kernel, count, sections, size, moments),...  27.9 us
    unnamed x2, local copies, waits for them, and re-layouts  1.31 us

profile of v3, /device:TPU:9, one launch (start us, length us, event | category | flops | bytes accessed | tf_op | source)
XLA Modules:
  0.0 29.9 jit_solution(8325601839878481197)
XLA Ops:
  0.6 27.9 %shard_map.86 = (f32[8,128,128]{2,1,0:T(8,128)S(1)}, f32[1,2]{1,0:T(1,128)S(1)}) custom-call(s32[1,8]{1,0:T(1,128)} %left_dims.1, s32[1,8]{1,0:T(1,128)} %right_dims.1, s32[1,8]{1,0:T(1,128)} %left_labels.1, s32[1,8]{1,0:T(1,128)} %right_labels.1, bf16[8,128,128]{2,1,0:T(8,128)(2,1)} %bitcast.7, bf16[256,128]{1,0:T(8,128)(2,1)} %bitcast.8, ...), custom_call_target="tpu_custom_call" | custom-call | tf_op jit(solution)/shard_map/pallas_call | solution.py:322
  28.6 0.8 %copy.12 = f32[1,8,128,1,128]{4,3,2,1,0:T(1,128)} copy(f32[1,8,128,1,128]{4,3,2,1,0:T(1,128)S(1)} %bitcast.6) | data formatting | bytes 1048576
  29.4 0.5 %copy.13 = f32[1,2]{1,0:T(1,128)} copy(f32[1,2]{1,0:T(1,128)S(1)} %get-tuple-element.9) | data formatting | bytes 16

commit v4 on v3

--- a/solution.py
+++ b/solution.py
@@ -129,7 +129,7 @@
         for w in range(TERMS):
             arrive(w)
             block = term(env.at[me], w)
-            for k in list(range(2, count, 2)) + [1]:
+            for k in list(range(count - 2, 0, -2)) + [1]:
                 copies[k, w] = copy_to(phase, k, k, block, block, w)
                 copies[k, w].start()
         for w in range(TERMS):
@@ -141,10 +141,9 @@
         for w in range(TERMS):
             for k in range(1, count, 2):
                 copies[k, w].wait_recv()
-        for key in copies:
-            copies[key].wait_send()
-
-    gather(0, first_env, lambda w: None)
+        return copies.values()
+
+    first_copies = gather(0, first_env, lambda w: None)
 
     @pl.when(jnp.logical_not(has_previous))
     def _():
@@ -282,7 +281,8 @@
 
     @pl.when(has_previous)
     def _():
-        gather(2, second_env, lambda w: onward[w].wait_recv())
+        for copy in gather(2, second_env, lambda w: onward[w].wait_recv()):
+            copy.wait_send()
 
     @pl.when(jnp.logical_not(has_previous))
     def _():
@@ -297,9 +297,9 @@
     lane = lax.broadcasted_iota(jnp.int32, (1, size), 1)
     energies_ref[...] = jnp.where(lane == 0, first_ritz, second_ritz)[:, :2]
 
-    for copies in (first_sums, second_sums):
-        for k in copies:
-            copies[k].wait_send()
+    for copies in (first_copies, first_sums.values(), second_sums.values()):
+        for copy in copies:
+            copy.wait_send()
 
     @pl.when(has_next)
     def _():

time: 30.1 us -> 29.1 us (0.967)
  Pallas kernels: 27.9 us -> 26.9 us
    pallas_call x1, Pallas kernels: 27.9 us -> 26.9 us  [local(): pl.pallas_call(functools.partial(kernel, count, sections, size, moments),...]
where the time goes in v4:
time: 29.1 us; the launch traced here: 28.9 us
  Pallas kernels  26.9 us (92%)
  local copies, waits for them, and re-layouts  1.31 us (5%)
  between operations  0.64 us (2%)
    pallas_call x1, Pallas kernels, local(): pl.pallas_call(functools.partial(kernel, count, sections, size, moments),...  26.9 us
    unnamed x2, local copies, waits for them, and re-layouts  1.31 us

profile of v4, /device:TPU:9, one launch (start us, length us, event | category | flops | bytes accessed | tf_op | source)
XLA Modules:
  0.0 28.9 jit_solution(2745676242164143000)
XLA Ops:
  0.6 26.9 %shard_map.86 = (f32[8,128,128]{2,1,0:T(8,128)S(1)}, f32[1,2]{1,0:T(1,128)S(1)}) custom-call(s32[1,8]{1,0:T(1,128)} %left_dims.1, s32[1,8]{1,0:T(1,128)} %right_dims.1, s32[1,8]{1,0:T(1,128)} %left_labels.1, s32[1,8]{1,0:T(1,128)} %right_labels.1, bf16[8,128,128]{2,1,0:T(8,128)(2,1)} %bitcast.7, bf16[256,128]{1,0:T(8,128)(2,1)} %bitcast.8, ...), custom_call_target="tpu_custom_call" | custom-call | tf_op jit(solution)/shard_map/pallas_call | solution.py:322
  27.6 0.8 %copy.12 = f32[1,8,128,1,128]{4,3,2,1,0:T(1,128)} copy(f32[1,8,128,1,128]{4,3,2,1,0:T(1,128)S(1)} %bitcast.6) | data formatting | bytes 1048576
  28.4 0.5 %copy.13 = f32[1,2]{1,0:T(1,128)} copy(f32[1,2]{1,0:T(1,128)S(1)} %get-tuple-element.9) | data formatting | bytes 16

commit v5 on v4

--- a/solution.py
+++ b/solution.py
@@ -124,26 +124,33 @@
     def term(ref, w):
         return ref.at[pl.ds(w * size, size)]
 
-    def gather(phase, env, arrive):
+    def routes(phase, env):
         copies = {}
         for w in range(TERMS):
-            arrive(w)
             block = term(env.at[me], w)
             for k in list(range(count - 2, 0, -2)) + [1]:
                 copies[k, w] = copy_to(phase, k, k, block, block, w)
+            for k in range(2, count, 2):
+                block = term(env.at[origin(me, k, count)], w)
+                copies[k + 1, w] = copy_to(phase, k + 1, 1, block, block, w)
+        return copies
+
+    def gather(copies, arrive):
+        for w in range(TERMS):
+            arrive(w)
+            for k in list(range(count - 2, 0, -2)) + [1]:
                 copies[k, w].start()
         for w in range(TERMS):
             for k in range(2, count, 2):
-                block = term(env.at[origin(me, k, count)], w)
                 copies[k, w].wait_recv()
-                copies[k + 1, w] = copy_to(phase, k + 1, 1, block, block, w)
                 copies[k + 1, w].start()
         for w in range(TERMS):
             for k in range(1, count, 2):
                 copies[k, w].wait_recv()
-        return copies.values()
-
-    first_copies = gather(0, first_env, lambda w: None)
+
+    first_copies = routes(0, first_env)
+    second_copies = routes(2, second_env)
+    gather(first_copies, lambda w: None)
 
     @pl.when(jnp.logical_not(has_previous))
     def _():
@@ -281,8 +288,7 @@
 
     @pl.when(has_previous)
     def _():
-        for copy in gather(2, second_env, lambda w: onward[w].wait_recv()):
-            copy.wait_send()
+        gather(second_copies, lambda w: onward[w].wait_recv())
 
     @pl.when(jnp.logical_not(has_previous))
     def _():
@@ -297,8 +303,13 @@
     lane = lax.broadcasted_iota(jnp.int32, (1, size), 1)
     energies_ref[...] = jnp.where(lane == 0, first_ritz, second_ritz)[:, :2]
 
-    for copies in (first_copies, first_sums.values(), second_sums.values()):
+    for copies in (first_copies.values(), first_sums.values(), second_sums.values()):
         for copy in copies:
+            copy.wait_send()
+
+    @pl.when(has_previous)
+    def _():
+        for copy in second_copies.values():
             copy.wait_send()
 
     @pl.when(has_next)

time: 29.1 us -> 28.7 us (0.986)
  Pallas kernels: 26.9 us -> 26.6 us
    pallas_call x1, Pallas kernels: 26.9 us -> 26.6 us  [local(): pl.pallas_call(functools.partial(kernel, count, sections, size, moments),...]
where the time goes in v5:
time: 28.7 us; the launch traced here: 28.5 us
  Pallas kernels  26.6 us (93%)
  local copies, waits for them, and re-layouts  1.31 us (5%)
  between operations  0.64 us (2%)
    pallas_call x1, Pallas kernels, local(): pl.pallas_call(functools.partial(kernel, count, sections, size, moments),...  26.6 us
    unnamed x2, local copies, waits for them, and re-layouts  1.31 us

profile of v5, /device:TPU:9, one launch (start us, length us, event | category | flops | bytes accessed | tf_op | source)
XLA Modules:
  0.0 28.5 jit_solution(2624989431854327001)
XLA Ops:
  0.6 26.6 %shard_map.86 = (f32[8,128,128]{2,1,0:T(8,128)S(1)}, f32[1,2]{1,0:T(1,128)S(1)}) custom-call(s32[1,8]{1,0:T(1,128)} %left_dims.1, s32[1,8]{1,0:T(1,128)} %right_dims.1, s32[1,8]{1,0:T(1,128)} %left_labels.1, s32[1,8]{1,0:T(1,128)} %right_labels.1, bf16[8,128,128]{2,1,0:T(8,128)(2,1)} %bitcast.7, bf16[256,128]{1,0:T(8,128)(2,1)} %bitcast.8, ...), custom_call_target="tpu_custom_call" | custom-call | tf_op jit(solution)/shard_map/pallas_call | solution.py:333
  27.2 0.8 %copy.12 = f32[1,8,128,1,128]{4,3,2,1,0:T(1,128)} copy(f32[1,8,128,1,128]{4,3,2,1,0:T(1,128)S(1)} %bitcast.6) | data formatting | bytes 1048576
  28.0 0.5 %copy.13 = f32[1,2]{1,0:T(1,128)} copy(f32[1,2]{1,0:T(1,128)S(1)} %get-tuple-element.9) | data formatting | bytes 16
